TPU v7x, 256 devices: a whole 4x4x8 slice. The times are simulated.
256 devices in a mesh: expert: 32 (over y, x, core), tensor: 8 (over z).
Axes of the slice: x: 4, y: 4, z: 8, core: 2. Of those that a mesh axis runs over, the one named last changes fastest.
Arguments:
- tokens: bfloat16 [16384, 4096], P('expert', 'tensor'), may hold values from -36 to 36
- expert_ids: int32 [16384, 1], P('expert'), may hold values from 0 to 63; in each aligned block of 512 rows (0 to 511, 512 to 1023, ...) at most 16 rows name the same one
- gates: float32 [16384, 1], P('expert'), may hold values from 0.25 to 1
- expert_in: bfloat16 [64, 4096, 2048], P('expert', 'tensor'), may hold values from -0.09375 to 0.09375
- expert_out: bfloat16 [64, 2048, 4096], P('expert', None, 'tensor'), may hold values from -0.125 to 0.125
- norm_gain: float32 [4096], replicated, may hold values from 0.5 to 2
- up_weight: bfloat16 [4096, 8192], P('expert', 'tensor'), may hold values from -0.09375 to 0.09375
- down_weight: bfloat16 [4096, 8192], P('expert', 'tensor'), may hold values from -0.0625 to 0.0625
Outputs:
- layer_output: bfloat16 [16384, 4096], P('expert', 'tensor')
Inputs may be any that keep to these rules, and one draw needn't show every extreme that they name: `expert_ids`: among the 512 tokens of one block, at most 16 carry the same expert id; in some blocks one id is carried by exactly 16 tokens.
All inputs are finite; a program needn't handle non-finite values.
Results may differ from a plain program's by a relative error of at most 0.015.
Values may be sent and summed in bfloat16 or wider, within the bound.
No kernel may reach another device: no remote copies, remote signals or barrier semaphores. Data moves between devices by JAX's collectives and lax.ppermute only.
A program may use at most 128 MiB of HBM per device.

v0:
```python
import jax
import jax.numpy as jnp
from jax import lax
from jax.sharding import PartitionSpec as P

EXP_DEV = 2


def slot_table(expert_col, experts, capacity):
    expert = expert_col[:, 0]
    onehot = (expert[:, None] == jnp.arange(experts, dtype=jnp.int32)[None, :]).astype(jnp.int32)
    before = jnp.cumsum(onehot, axis=0) - onehot
    position = jnp.sum(before * onehot, axis=1)
    slot_index = expert * capacity + position
    selector = jnp.arange(experts * capacity, dtype=jnp.int32)[:, None] == slot_index[None, :]
    return selector.astype(jnp.bfloat16)


def trade(buffer):
    result = lax.all_to_all(buffer, "expert", split_axis=0, concat_axis=0, tiled=True)
    return result


def gather_rows(weight, combine, start_value):
    return combine(start_value, lax.all_gather(weight, "expert", axis=0, tiled=True), jnp.int32(0))


def shards(tokens, expert_ids, gates, expert_in, expert_out, norm_gain, up_weight, down_weight):
    token_count = tokens.shape[0]
    local_width = tokens.shape[1]
    groups = lax.axis_size("expert")
    experts = EXP_DEV * groups
    capacity = 2 * token_count // experts
    selector = slot_table(expert_ids, experts, capacity)
    outgoing = jnp.dot(selector, tokens, preferred_element_type=jnp.float32).astype(jnp.bfloat16)
    outgoing = outgoing.reshape(groups, EXP_DEV, capacity, local_width)
    arrived = trade(outgoing)
    partial_value = jnp.einsum(
        "sjcd,jdh->sjch", arrived, expert_in, preferred_element_type=jnp.float32
    )
    summed = lax.psum(partial_value.astype(jnp.bfloat16), "tensor").astype(jnp.float32)
    active = jax.nn.relu(summed).astype(jnp.bfloat16)
    produced = jnp.einsum(
        "sjch,jhd->sjcd", active, expert_out, preferred_element_type=jnp.float32
    ).astype(jnp.bfloat16)
    returned = trade(produced).reshape(experts * capacity, local_width)
    routed = lax.dot_general(
        selector, returned, (((0,), (0,)), ((), ())), preferred_element_type=jnp.float32
    )
    mixed = (tokens.astype(jnp.float32) + gates * routed).astype(jnp.bfloat16)
    whole = lax.all_gather(mixed, "tensor", axis=1, tiled=True)
    whole_f32 = whole.astype(jnp.float32)
    mean_square = jnp.mean(whole_f32 * whole_f32, axis=1, keepdims=True)
    normed = (whole_f32 * lax.rsqrt(mean_square + 1e-06) * norm_gain).astype(jnp.bfloat16)

    def add_up(carry, piece, start):
        return jnp.dot(normed, piece, preferred_element_type=jnp.float32)

    ffn_hidden = gather_rows(
        up_weight, add_up, jnp.zeros((token_count, up_weight.shape[1]), jnp.float32)
    )
    ffn_active = jax.nn.gelu(ffn_hidden, approximate=True).astype(jnp.bfloat16)

    def add_down(carry, piece, start):
        contribution = lax.dot_general(
            ffn_active, piece, (((1,), (1,)), ((), ())), preferred_element_type=jnp.float32
        )
        return contribution

    outputs = gather_rows(
        down_weight, add_down, jnp.zeros((token_count, whole.shape[1]), jnp.float32)
    )
    summed_out = lax.psum_scatter(
        outputs.astype(jnp.bfloat16), "tensor", scatter_dimension=1, tiled=True
    ).astype(jnp.float32)
    return (mixed.astype(jnp.float32) + summed_out).astype(jnp.bfloat16)


def solution(mesh):
    return jax.shard_map(
        shards,
        mesh=mesh,
        in_specs=(
            P("expert", "tensor"),
            P("expert", None),
            P("expert", None),
            P("expert", "tensor", None),
            P("expert", None, "tensor"),
            P(),
            P("expert", "tensor"),
            P("expert", "tensor"),
        ),
        out_specs=P("expert", "tensor"),
        check_vma=False,
    )
```

profile of v0, /device:TPU:1, one launch (start us, length us, event | category | flops | bytes accessed | tf_op | source)
XLA Modules:
  0.0 424.8 jit_solution(10991581283528540992)
XLA Ops:
  6.5 0.0 all-reduce.2.cloned.1.call-start
  6.5 0.7 fusion.42
  7.2 1.2 reduce-window.6
  8.4 0.2 slice_reduce_fusion
  8.7 0.0 copy-start.1
  8.7 0.9 fusion.41
  9.7 0.9 multiply_add_fusion
  10.6 1.8 fusion.24
  12.4 25.6 %all_to_all.10 = bf16[32,2,16,512]{3,2,1,0:T(8,128)(2,1)S(1)} all-to-all(bf16[32,2,16,512]{3,2,1,0:T(8,128)(2,1)S(1)} %bitcast.50), channel_id=1, replica_groups=mesh['expert'=32,'tensor'=8] {'expert'}, dimensions={0} | all-to-all | bytes 2097152 | tf_op jit(solution)/shard_map/all_to_all | solution.py:20
  37.9 0.0 copy-done.1
  37.9 4.3 %convert_bitcast_fusion = bf16[32,2,16,2048]{3,2,0,1:T(8,128)(2,1)} fusion(bf16[2,512,2048]{2,1,0:T(8,128)(2,1)S(1)} %copy-done.1, bf16[32,2,16,512]{3,2,1,0:T(8,128)(2,1)S(1)} %all_to_all.10), kind=kOutput, calls=%fused_computation.15 | convolution fusion | flops 2149580800 | bytes 9437184 | tf_op jit(solution)/shard_map/sjcd,jdh->sjch/dot_general | solution.py:38
  42.2 0.0 all-reduce.2.cloned.1.call-update
  42.3 0.0 all-gather.4.cloned.1.call-start
  42.3 108.1 %all-reduce.2.cloned.1.call-done = bf16[32,2,16,2048]{3,2,0,1:T(8,128)(2,1)} async-done(((bf16[32,2,16,2048]{3,2,0,1:T(8,128)(2,1)}), bf16[32,2,16,2048]{3,2,0,1:T(8,128)(2,1)}) %all-reduce.2.cloned.1.call-update) | async-done | bytes 4194320 | tf_op jit(solution)/shard_map/psum | solution.py:41
  150.4 5.8 %fusion.30 = bf16[32,2,16,512]{3,2,0,1:T(8,128)(2,1)S(1)} fusion(bf16[2,2048,512]{2,1,0:T(8,128)(2,1)} %param.12, bf16[32,2,16,2048]{3,2,0,1:T(8,128)(2,1)} %all-reduce.2.cloned.1.call-done), kind=kOutput, calls=%fused_computation.30 | convolution fusion | flops 2154299392 | bytes 9437184 | tf_op jit(solution)/shard_map/sjch,jhd->sjcd/dot_general | solution.py:43
  156.2 0.0 copy-start.2
  156.2 0.0 copy-start.4
  156.2 0.1 copy.16
  156.3 24.6 %all_to_all.11 = bf16[32,2,16,512]{3,2,1,0:T(8,128)(2,1)S(1)} all-to-all(bf16[32,2,16,512]{3,2,1,0:T(8,128)(2,1)S(1)} %copy.16), channel_id=1, replica_groups=mesh['expert'=32,'tensor'=8] {'expert'}, dimensions={0} | all-to-all | bytes 2097152 | tf_op jit(solution)/shard_map/all_to_all | solution.py:20
  180.9 0.0 copy-done.2
  180.9 0.0 copy-done.4
  180.9 0.0 copy-start.3
  180.9 1.6 fusion.35
  182.5 0.0 all-gather.4.cloned.1.call-update
  182.5 0.0 all-gather.6.cloned.1.call-start
  182.6 0.7 all-gather.6.cloned.1.call-update
  183.3 0.0 all-gather.8.cloned.1.call-start
  183.3 0.5 all-gather.8.cloned.1.call-update
  183.8 0.2 reduce-scatter.2.cloned.1.call-start
  184.1 48.4 %all-gather.4.cloned.1.call-done = bf16[512,4096]{1,0:T(8,128)(2,1)} async-done(((bf16[512,512]{1,0:T(8,128)(2,1)}), bf16[512,4096]{1,0:T(8,128)(2,1)}) %all-gather.4.cloned.1.call-update) | async-done | bytes 4194320 | tf_op jit(solution)/shard_map/all_gather | solution.py:51
  232.4 3.1 fusion
  235.5 56.4 %all-gather.6.cloned.1.call-done = bf16[4096,1024]{1,0:T(8,128)(2,1)} async-done(((bf16[128,1024]{1,0:T(8,128)(2,1)}), bf16[4096,1024]{1,0:T(8,128)(2,1)}) %all-gather.6.cloned.1.call-update) | async-done | bytes 8388624 | tf_op jit(solution)/shard_map/all_gather | solution.py:25
  292.0 0.0 copy-done.3
  292.0 9.6 %fusion.21 = bf16[512,1024]{1,0:T(8,128)(2,1)S(1)} fusion(bf16[4096,1024]{1,0:T(8,128)(2,1)} %all-gather.6.cloned.1.call-done, bf16[512,4096]{1,0:T(8,128)(2,1)} %all-gather.4.cloned.1.call-done, f32[4096]{0:T(1024)S(1)} %copy-done.3, f32[512]{0:T(512)S(1)} %add_rsqrt_fusion), kind=kOutput, calls=%fused_computation.24 | convolution fusion | flops 4308074496 | bytes 13649920 | tf_op jit(solution)/shard_map/dot_general | solution.py:57
  301.6 50.4 %all-gather.8.cloned.1.call-done = bf16[4096,1024]{1,0:T(8,128)(2,1)} async-done(((bf16[128,1024]{1,0:T(8,128)(2,1)}), bf16[4096,1024]{1,0:T(8,128)(2,1)}) %all-gather.8.cloned.1.call-update) | async-done | bytes 8388624 | tf_op jit(solution)/shard_map/all_gather | solution.py:25
  352.0 9.5 %convolution_convert_fusion = bf16[512,4096]{1,0:T(8,128)(2,1)} fusion(bf16[512,1024]{1,0:T(8,128)(2,1)S(1)} %fusion.21, bf16[4096,1024]{1,0:T(8,128)(2,1)} %all-gather.8.cloned.1.call-done), kind=kOutput, calls=%fused_computation.6 | convolution fusion | flops 4297064448 | bytes 13631488 | tf_op jit(solution)/shard_map/dot_general | solution.py:65
  361.5 0.0 copy-start
  361.5 0.0 reduce-scatter.2.cloned.1.call-update
  361.5 54.7 %reduce-scatter.2.cloned.1.call-done = bf16[512,512]{1,0:T(8,128)(2,1)} async-done(((bf16[512,4096]{1,0:T(8,128)(2,1)}), bf16[512,512]{1,0:T(8,128)(2,1)}) %reduce-scatter.2.cloned.1.call-update) | async-done | bytes 524304 | tf_op jit(solution)/shard_map/reduce_scatter | solution.py:73
  416.3 0.0 copy-done
  416.3 2.0 add_convert_fusion
  (3 shorter events, 0.0 us)
Async XLA Ops:
  6.5 143.8 %all-reduce.2.cloned.1.call-start = ((), (), s32[]{:S(2)}) async-start(), calls=%async_computation.3 | async-start | bytes 8388608 | tf_op jit(solution)/shard_map/psum | solution.py:41
  8.7 29.2 %copy-start.1 = (bf16[2,512,2048]{2,1,0:T(8,128)(2,1)S(1)}, bf16[2,512,2048]{2,1,0:T(8,128)(2,1)}, u32[]{:S(2)}) copy-start(bf16[2,512,2048]{2,1,0:T(8,128)(2,1)} %param.11) | copy-start | bytes 12582916
  42.3 190.2 %all-gather.4.cloned.1.call-start = ((), (), s32[]{:S(2)}) async-start(), calls=%async_computation.4 | async-start | bytes 4718592 | tf_op jit(solution)/shard_map/all_gather | solution.py:51
  156.2 24.7 %copy-start.2 = (bf16[512,512]{1,0:T(8,128)(2,1)S(1)}, bf16[512,512]{1,0:T(8,128)(2,1)}, u32[]{:S(2)}) copy-start(bf16[512,512]{1,0:T(8,128)(2,1)} %param.8) | copy-start | bytes 1572868
  156.2 24.7 %copy-start.4 = (f32[512,1]{0,1:T(1,128)S(1)}, f32[512,1]{0,1:T(1,128)}, u32[]{:S(2)}) copy-start(f32[512,1]{0,1:T(1,128)} %param.10) | copy-start | bytes 6148
  180.9 111.0 %copy-start.3 = (f32[4096]{0:T(1024)S(1)}, f32[4096]{0:T(1024)}, u32[]{:S(2)}) copy-start(f32[4096]{0:T(1024)} %param.13) | copy-start | bytes 49156
  182.5 109.4 %all-gather.6.cloned.1.call-start = ((), (), s32[]{:S(2)}) async-start(), calls=%async_computation.5 | async-start | bytes 8650752 | tf_op jit(solution)/shard_map/all_gather | solution.py:25
  183.3 168.7 %all-gather.8.cloned.1.call-start = ((), (), s32[]{:S(2)}) async-start(), calls=%async_computation.6 | async-start | bytes 8650752 | tf_op jit(solution)/shard_map/all_gather | solution.py:25
  183.8 232.4 %reduce-scatter.2.cloned.1.call-start = ((), (), s32[]{:S(2)}) async-start(), calls=%async_computation.7 | async-start | bytes 4718592 | tf_op jit(solution)/shard_map/reduce_scatter | solution.py:73
  361.5 54.8 %copy-start = (bf16[512,512]{1,0:T(8,128)(2,1)S(1)}, bf16[512,512]{1,0:T(8,128)(2,1)}, u32[]{:S(2)}) copy-start(bf16[512,512]{1,0:T(8,128)(2,1)} %fusion.35) | copy-start | bytes 1572868
Sparse Core Ops, SparseCore 0:
  42.4 107.9 all-reduce.1
  182.6 49.7 all-gather.3
  235.0 56.9 all-gather.5
  294.4 57.5 all-gather.7
  361.6 54.5 reduce-scatter.1
where the time goes:
time: 425 us
  waiting for transfers between devices  319 us (75%)
  blocking collectives  50.2 us (12%)
  matrix products  32.6 us (8%)
  between operations  13.2 us (3%)
  other arithmetic  8.86 us (2%)
    psum x1, waiting for transfers between devices, shards(): lax.psum(partial_value.astype(jnp.bfloat16), 'tensor').astype(jnp.float32)  108 us
    all_gather x2, waiting for transfers between devices, gather_rows(): lax.all_gather(weight, 'expert', axis=0, tiled=True)  107 us
    reduce_scatter x1, waiting for transfers between devices, shards(): lax.psum_scatter(outputs.astype(jnp.bfloat16), 'tensor', scatter_dimensio...  54.7 us
    all_to_all x2, blocking collectives, trade(): lax.all_to_all(buffer, 'expert', split_axis=0, concat_axis=0, tiled=True)  50.2 us
    all_gather x1, waiting for transfers between devices, shards(): whole = lax.all_gather(mixed, 'tensor', axis=1, tiled=True)  48.4 us
    dot_general x1, matrix products, add_up(): return jnp.dot(normed, piece, preferred_element_type=jnp.float32)  9.58 us
    dot_general x1, matrix products, add_down(): lax.dot_general(ffn_active, piece, (((1,), (1,)), ((), ())), preferred_el...  9.54 us
  transfers between devices with their start and end apart: 5, of which 5 were waited for; matrix products, arithmetic and copies ran while one was open for 3% of the time, Pallas kernels for 0%

commit v1 on v0

--- a/solution.py
+++ b/solution.py
@@ -8,9 +8,10 @@
 
 def slot_table(expert_col, experts, capacity):
     expert = expert_col[:, 0]
-    onehot = (expert[:, None] == jnp.arange(experts, dtype=jnp.int32)[None, :]).astype(jnp.int32)
-    before = jnp.cumsum(onehot, axis=0) - onehot
-    position = jnp.sum(before * onehot, axis=1)
+    count = expert.shape[0]
+    order = jnp.arange(count, dtype=jnp.int32)
+    same = (expert[:, None] == expert[None, :]) & (order[None, :] < order[:, None])
+    position = jnp.sum(same.astype(jnp.int32), axis=1)
     slot_index = expert * capacity + position
     selector = jnp.arange(experts * capacity, dtype=jnp.int32)[:, None] == slot_index[None, :]
     return selector.astype(jnp.bfloat16)

time: 425 us -> 423 us (level)
  no operation moved by 1% of the time
where the time goes in v1:
time: 423 us
  waiting for transfers between devices  319 us (75%)
  blocking collectives  50.2 us (12%)
  matrix products  32.6 us (8%)
  between operations  13.2 us (3%)
  other arithmetic  7.03 us (2%)
    psum x1, waiting for transfers between devices, shards(): lax.psum(partial_value.astype(jnp.bfloat16), 'tensor').astype(jnp.float32)  108 us
    all_gather x2, waiting for transfers between devices, gather_rows(): lax.all_gather(weight, 'expert', axis=0, tiled=True)  107 us
    reduce_scatter x1, waiting for transfers between devices, shards(): lax.psum_scatter(outputs.astype(jnp.bfloat16), 'tensor', scatter_dimensio...  54.7 us
    all_to_all x2, blocking collectives, trade(): lax.all_to_all(buffer, 'expert', split_axis=0, concat_axis=0, tiled=True)  50.2 us
    all_gather x1, waiting for transfers between devices, shards(): whole = lax.all_gather(mixed, 'tensor', axis=1, tiled=True)  48.4 us
    dot_general x1, matrix products, add_up(): return jnp.dot(normed, piece, preferred_element_type=jnp.float32)  9.58 us
    dot_general x1, matrix products, add_down(): lax.dot_general(ffn_active, piece, (((1,), (1,)), ((), ())), preferred_el...  9.57 us
  transfers between devices with their start and end apart: 5, of which 5 were waited for; matrix products, arithmetic and copies ran while one was open for 3% of the time, Pallas kernels for 0%

profile of v1, /device:TPU:1, one launch (start us, length us, event | category | flops | bytes accessed | tf_op | source)
XLA Modules:
  0.0 422.7 jit_solution(1282529528484603267)
XLA Ops:
  6.5 0.0 all-reduce.2.cloned.1.call-start
  6.5 0.0 copy-start.1
  6.5 1.1 convert_reduce_fusion
  7.6 0.9 multiply_add_fusion
  8.5 1.8 fusion.24
  10.3 25.6 %all_to_all.10 = bf16[32,2,16,512]{3,2,1,0:T(8,128)(2,1)S(1)} all-to-all(bf16[32,2,16,512]{3,2,1,0:T(8,128)(2,1)S(1)} %bitcast.30), channel_id=1, replica_groups=mesh['expert'=32,'tensor'=8] {'expert'}, dimensions={0} | all-to-all | bytes 2097152 | tf_op jit(solution)/shard_map/all_to_all | solution.py:21
  35.8 0.0 copy-done.1
  35.8 4.3 %convert_bitcast_fusion = bf16[32,2,16,2048]{3,2,0,1:T(8,128)(2,1)} fusion(bf16[2,512,2048]{2,1,0:T(8,128)(2,1)S(1)} %copy-done.1, bf16[32,2,16,512]{3,2,1,0:T(8,128)(2,1)S(1)} %all_to_all.10), kind=kOutput, calls=%fused_computation.15 | convolution fusion | flops 2149580800 | bytes 9437184 | tf_op jit(solution)/shard_map/sjcd,jdh->sjch/dot_general | solution.py:39
  40.2 0.0 all-reduce.2.cloned.1.call-update
  40.2 0.0 all-gather.4.cloned.1.call-start
  40.2 108.1 %all-reduce.2.cloned.1.call-done = bf16[32,2,16,2048]{3,2,0,1:T(8,128)(2,1)} async-done(((bf16[32,2,16,2048]{3,2,0,1:T(8,128)(2,1)}), bf16[32,2,16,2048]{3,2,0,1:T(8,128)(2,1)}) %all-reduce.2.cloned.1.call-update) | async-done | bytes 4194320 | tf_op jit(solution)/shard_map/psum | solution.py:42
  148.3 5.8 %fusion.30 = bf16[32,2,16,512]{3,2,0,1:T(8,128)(2,1)S(1)} fusion(bf16[2,2048,512]{2,1,0:T(8,128)(2,1)} %param.12, bf16[32,2,16,2048]{3,2,0,1:T(8,128)(2,1)} %all-reduce.2.cloned.1.call-done), kind=kOutput, calls=%fused_computation.30 | convolution fusion | flops 2154299392 | bytes 9437184 | tf_op jit(solution)/shard_map/sjch,jhd->sjcd/dot_general | solution.py:44
  154.1 0.0 copy-start.2
  154.1 0.0 copy-start.4
  154.1 0.1 copy.15
  154.2 24.6 %all_to_all.11 = bf16[32,2,16,512]{3,2,1,0:T(8,128)(2,1)S(1)} all-to-all(bf16[32,2,16,512]{3,2,1,0:T(8,128)(2,1)S(1)} %copy.15), channel_id=1, replica_groups=mesh['expert'=32,'tensor'=8] {'expert'}, dimensions={0} | all-to-all | bytes 2097152 | tf_op jit(solution)/shard_map/all_to_all | solution.py:21
  178.8 0.0 copy-done.2
  178.9 0.0 copy-done.4
  178.9 0.0 copy-start.3
  178.9 1.6 fusion.35
  180.4 0.0 all-gather.4.cloned.1.call-update
  180.5 0.0 all-gather.6.cloned.1.call-start
  180.5 0.7 all-gather.6.cloned.1.call-update
  181.2 0.0 all-gather.8.cloned.1.call-start
  181.2 0.5 all-gather.8.cloned.1.call-update
  181.8 0.2 reduce-scatter.2.cloned.1.call-start
  182.0 48.4 %all-gather.4.cloned.1.call-done = bf16[512,4096]{1,0:T(8,128)(2,1)} async-done(((bf16[512,512]{1,0:T(8,128)(2,1)}), bf16[512,4096]{1,0:T(8,128)(2,1)}) %all-gather.4.cloned.1.call-update) | async-done | bytes 4194320 | tf_op jit(solution)/shard_map/all_gather | solution.py:52
  230.4 3.1 fusion
  233.4 56.4 %all-gather.6.cloned.1.call-done = bf16[4096,1024]{1,0:T(8,128)(2,1)} async-done(((bf16[128,1024]{1,0:T(8,128)(2,1)}), bf16[4096,1024]{1,0:T(8,128)(2,1)}) %all-gather.6.cloned.1.call-update) | async-done | bytes 8388624 | tf_op jit(solution)/shard_map/all_gather | solution.py:26
  289.9 0.0 copy-done.3
  289.9 9.6 %fusion.21 = bf16[512,1024]{1,0:T(8,128)(2,1)S(1)} fusion(bf16[4096,1024]{1,0:T(8,128)(2,1)} %all-gather.6.cloned.1.call-done, bf16[512,4096]{1,0:T(8,128)(2,1)} %all-gather.4.cloned.1.call-done, f32[4096]{0:T(1024)S(1)} %copy-done.3, f32[512]{0:T(512)S(1)} %add_rsqrt_fusion), kind=kOutput, calls=%fused_computation.24 | convolution fusion | flops 4308074496 | bytes 13649920 | tf_op jit(solution)/shard_map/dot_general | solution.py:58
  299.5 50.4 %all-gather.8.cloned.1.call-done = bf16[4096,1024]{1,0:T(8,128)(2,1)} async-done(((bf16[128,1024]{1,0:T(8,128)(2,1)}), bf16[4096,1024]{1,0:T(8,128)(2,1)}) %all-gather.8.cloned.1.call-update) | async-done | bytes 8388624 | tf_op jit(solution)/shard_map/all_gather | solution.py:26
  349.9 9.6 %convolution_convert_fusion = bf16[512,4096]{1,0:T(8,128)(2,1)} fusion(bf16[512,1024]{1,0:T(8,128)(2,1)S(1)} %fusion.21, bf16[4096,1024]{1,0:T(8,128)(2,1)} %all-gather.8.cloned.1.call-done), kind=kOutput, calls=%fused_computation.6 | convolution fusion | flops 4297064448 | bytes 13631488 | tf_op jit(solution)/shard_map/dot_general | solution.py:66
  359.5 0.0 copy-start
  359.5 0.0 reduce-scatter.2.cloned.1.call-update
  359.5 54.7 %reduce-scatter.2.cloned.1.call-done = bf16[512,512]{1,0:T(8,128)(2,1)} async-done(((bf16[512,4096]{1,0:T(8,128)(2,1)}), bf16[512,512]{1,0:T(8,128)(2,1)}) %reduce-scatter.2.cloned.1.call-update) | async-done | bytes 524304 | tf_op jit(solution)/shard_map/reduce_scatter | solution.py:74
  414.2 0.0 copy-done
  414.2 2.0 add_convert_fusion
  (1 shorter events, 0.0 us)
Async XLA Ops:
  6.5 141.8 %all-reduce.2.cloned.1.call-start = ((), (), s32[]{:S(2)}) async-start(), calls=%async_computation.3 | async-start | bytes 8388608 | tf_op jit(solution)/shard_map/psum | solution.py:42
  6.5 29.3 %copy-start.1 = (bf16[2,512,2048]{2,1,0:T(8,128)(2,1)S(1)}, bf16[2,512,2048]{2,1,0:T(8,128)(2,1)}, u32[]{:S(2)}) copy-start(bf16[2,512,2048]{2,1,0:T(8,128)(2,1)} %param.11) | copy-start | bytes 12582916
  40.2 190.2 %all-gather.4.cloned.1.call-start = ((), (), s32[]{:S(2)}) async-start(), calls=%async_computation.4 | async-start | bytes 4718592 | tf_op jit(solution)/shard_map/all_gather | solution.py:52
  154.1 24.7 %copy-start.2 = (bf16[512,512]{1,0:T(8,128)(2,1)S(1)}, bf16[512,512]{1,0:T(8,128)(2,1)}, u32[]{:S(2)}) copy-start(bf16[512,512]{1,0:T(8,128)(2,1)} %param.8) | copy-start | bytes 1572868
  154.1 24.7 %copy-start.4 = (f32[512,1]{0,1:T(1,128)S(1)}, f32[512,1]{0,1:T(1,128)}, u32[]{:S(2)}) copy-start(f32[512,1]{0,1:T(1,128)} %param.10) | copy-start | bytes 6148
  178.9 111.0 %copy-start.3 = (f32[4096]{0:T(1024)S(1)}, f32[4096]{0:T(1024)}, u32[]{:S(2)}) copy-start(f32[4096]{0:T(1024)} %param.13) | copy-start | bytes 49156
  180.5 109.4 %all-gather.6.cloned.1.call-start = ((), (), s32[]{:S(2)}) async-start(), calls=%async_computation.5 | async-start | bytes 8650752 | tf_op jit(solution)/shard_map/all_gather | solution.py:26
  181.2 168.7 %all-gather.8.cloned.1.call-start = ((), (), s32[]{:S(2)}) async-start(), calls=%async_computation.6 | async-start | bytes 8650752 | tf_op jit(solution)/shard_map/all_gather | solution.py:26
  181.8 232.5 %reduce-scatter.2.cloned.1.call-start = ((), (), s32[]{:S(2)}) async-start(), calls=%async_computation.7 | async-start | bytes 4718592 | tf_op jit(solution)/shard_map/reduce_scatter | solution.py:74
  359.5 54.8 %copy-start = (bf16[512,512]{1,0:T(8,128)(2,1)S(1)}, bf16[512,512]{1,0:T(8,128)(2,1)}, u32[]{:S(2)}) copy-start(bf16[512,512]{1,0:T(8,128)(2,1)} %fusion.35) | copy-start | bytes 1572868
Sparse Core Ops, SparseCore 0:
  40.3 107.9 all-reduce.1
  180.6 49.7 all-gather.3
  232.9 56.9 all-gather.5
  292.3 57.5 all-gather.7
  359.6 54.5 reduce-scatter.1
